TPU v7x, 32 devices: a whole 2x2x4 slice. The times are simulated.
32 devices in a mesh: group: 4 (over y, core), shard: 8 (over z, x).
Axes of the slice: x: 2, y: 2, z: 4, core: 2. Of those that a mesh axis runs over, the one named last changes fastest.
Arguments:
- embeddings: bfloat16 [16384, 1024], P(('group', 'shard')), may hold values from -30 to 30
- destinations: int32 [2048, 1], P(('group', 'shard')), may hold values from 0 to 7; in each aligned block of 64 rows (0 to 63, 64 to 127, ...) at most 12 rows name the same one
- means: float32 [1024], replicated, may hold values from -0.5 to 0.5
- scales: float32 [1024], replicated, may hold values from 0.01 to 0.1
Outputs:
- codes: int32 [24576, 128], P(('group', 'shard'))
- quantized: bfloat16 [24576, 1024], P(('group', 'shard'))
- statistics: float32 [2, 1024], replicated
Inputs may be any that keep to these rules, and one draw needn't show every extreme that they name: `destinations`: within the 64 blocks of one device, no owner is named by more than 12 blocks.
All inputs are finite; a program needn't handle non-finite values.
Results may differ from a plain program's by a relative error of at most 0.0015.
Values may be sent and summed in bfloat16 or wider, within the bound.
A program may use at most 64 MiB of HBM per device.

v0:
```python
import jax
import jax.numpy as jnp
from jax import lax
from jax.sharding import PartitionSpec as P

BLOCK_ROWS = 8


def encode(rows, live, means, scales):
    centered = rows.astype(jnp.float32) - means
    bits = (centered > 0).astype(jnp.int32)
    bits = bits.reshape(rows.shape[:-1] + (rows.shape[-1] // 8, 8))
    weights = jnp.left_shift(jnp.int32(1), jnp.arange(8, dtype=jnp.int32))
    codes = jnp.sum(bits * weights, axis=-1) * live[..., None]
    quant = jnp.clip(centered / scales, -127.0, 127.0) * live[..., None].astype(jnp.float32)
    return (codes.astype(jnp.int32), quant.astype(jnp.bfloat16))


def body(embeddings, destinations, means, scales):
    owners_count = lax.axis_size("shard")
    width = embeddings.shape[1]
    blocks = embeddings.shape[0] // BLOCK_ROWS
    peer_cap = max(2, 3 * blocks // (2 * owners_count))
    owner = destinations[:, 0]
    order = jnp.arange(blocks, dtype=jnp.int32)
    same = owner[:, None] == owner[None, :]
    earlier = order[None, :] < order[:, None]
    slot = jnp.sum((same & earlier).astype(jnp.int32), axis=1)
    target = owner * peer_cap + slot
    places = jnp.arange(owners_count * peer_cap, dtype=jnp.int32)[:, None] == target[None, :]
    placed = jnp.dot(
        places.astype(jnp.bfloat16),
        embeddings.reshape(blocks, BLOCK_ROWS * width),
        preferred_element_type=jnp.float32,
    ).astype(jnp.bfloat16)
    placed = placed.reshape(owners_count, peer_cap, BLOCK_ROWS, width)
    flags = jnp.sum(places.astype(jnp.int32), axis=1).reshape(owners_count, peer_cap)
    sums = jnp.sum(embeddings, axis=0, dtype=jnp.float32)
    squares = jnp.sum(jnp.square(embeddings.astype(jnp.float32)), axis=0)
    within = lax.psum((sums, squares), "shard")
    sums, squares = lax.psum((within[0], within[1]), "group")
    arrived, arrived_flags = (
        lax.all_to_all(placed, "shard", split_axis=0, concat_axis=0, tiled=True),
        lax.all_to_all(flags, "shard", split_axis=0, concat_axis=0, tiled=True),
    )
    live_rows = jnp.broadcast_to(arrived_flags[..., None], arrived_flags.shape + (BLOCK_ROWS,))
    codes, quant = encode(arrived, live_rows, means, scales)
    return (codes.reshape(-1, width // 8), quant.reshape(-1, width), jnp.stack([sums, squares]))


def solution(mesh):
    in_specs = (P(("group", "shard"), None), P(("group", "shard"), None), P(), P())
    out_specs = (P(("group", "shard"), None), P(("group", "shard"), None), P())
    return jax.shard_map(body, mesh=mesh, in_specs=in_specs, out_specs=out_specs, check_vma=False)
```

profile of v0, /device:TPU:12, one launch (start us, length us, event | category | flops | bytes accessed | tf_op | source)
XLA Modules:
  0.0 121.2 jit_solution(7301879513745632336)
XLA Ops:
  0.6 0.9 convert_reduce_fusion.2
  1.5 0.7 multiply_add_fusion
  2.2 0.1 convert_reduce_fusion.1
  2.3 0.7 all_to_all.12
  3.0 6.3 %all-to-all-start.1 = ((s32[8,1,12]{2,1,0:T(1,128)}), s32[8,1,12]{2,1,0:T(1,128)S(1)}, u32[]{:S(2)}, u32[]{:S(2)}) async-start(s32[8,1,12]{2,1,0:T(1,128)} %bitcast.2), calls=%async_computation.1 | async-start | bytes 8192 | tf_op jit(solution)/shard_map/all_to_all | solution.py:44
  9.2 1.6 %reshape.50 = bf16[64,8192]{1,0:T(8,128)(2,1)S(1)} reshape(bf16[512,1024]{1,0:T(8,128)(2,1)} %param.4) | data formatting | bytes 2097152 | tf_op jit(solution)/shard_map/reshape | solution.py:33
  10.8 0.7 convolution_convert_fusion
  11.5 0.0 copy-start
  11.5 0.0 copy-start.1
  11.5 2.1 %copy.9 = bf16[12,8,8,1024]{3,2,1,0:T(8,128)(2,1)} copy(bf16[12,8,8,1024]{3,1,2,0:T(8,128)(2,1)S(1)} %bitcast.15) | data formatting | bytes 3145728
  13.6 0.5 all-to-all-done.1
  14.1 5.5 %all-to-all-start = ((bf16[8,12,8,1024]{3,2,1,0:T(8,128)(2,1)}), bf16[8,12,8,1024]{3,2,1,0:T(8,128)(2,1)S(1)}, u32[]{:S(2)}, u32[]{:S(2)}) async-start(bf16[8,12,8,1024]{3,2,1,0:T(8,128)(2,1)} %bitcast.9), calls=%async_computation | async-start | bytes 3145728 | tf_op jit(solution)/shard_map/all_to_all | solution.py:43
  19.6 0.0 copy-done
  19.6 0.3 convert_reduce_fusion
  19.9 44.3 %all-reduce = (f32[1024]{0:T(1024)S(1)}, f32[1024]{0:T(1024)S(1)}) all-reduce(f32[1024]{0:T(1024)S(1)} %get-tuple-element.4, f32[1024]{0:T(1024)S(1)} %get-tuple-element.3), channel_id=1, replica_groups=mesh['group'=4,'shard'=8] {'shard'}, use_global_device_ids=true, to_apply=%region_7.0 | all-reduce | flops 2048 | bytes 16384 | tf_op jit(solution)/shard_map/psum | solution.py:40
  64.2 6.0 %all-reduce.1 = (f32[1,1024]{1,0:T(1,128)S(1)}, f32[1,1024]{1,0:T(1,128)S(1)}) all-reduce(f32[1,1024]{1,0:T(1,128)S(1)} %bitcast.19, f32[1,1024]{1,0:T(1,128)S(1)} %bitcast.20), channel_id=1, replica_groups=mesh['group'=4,'shard'=8] {'group'}, use_global_device_ids=true, to_apply=%region_8.0 | all-reduce | flops 2048 | bytes 16384 | tf_op jit(solution)/shard_map/psum | solution.py:41
  70.2 0.6 pad_maximum_fusion
  70.8 0.1 mul_broadcast_in_dim_broadcast_in_dim.9
  70.9 0.1 mul_broadcast_in_dim_broadcast_in_dim.10
  71.0 0.0 all-to-all-done
  71.0 0.0 copy-done.1
  71.0 0.6 fusion
  71.6 31.5 %reshape.52 = pred[8,12,8,128,8]{4,3,2,1,0:T(8,128)(4,1)} reshape(pred[8,12,8,1024]{3,2,1,0:T(8,128)(4,1)S(1)} %fusion) | data formatting | bytes 1572864 | tf_op jit(solution)/shard_map/reshape | solution.py:12
  103.2 0.0 copy-start.2
  103.2 15.4 %select_reduce_fusion = s32[8,12,8,128]{3,2,1,0:T(8,128)S(1)} fusion(pred[8,12,8,128,8]{4,3,2,1,0:T(8,128)(4,1)} %reshape.52, s32[8]{0:T(128)S(1)} %iota_shift-left_fusion), kind=kLoop, calls=%fused_computation | loop fusion | flops 1474560 | bytes 1179680 | tf_op jit(solution)/shard_map/reduce_sum | solution.py:14
  118.5 0.9 bitcast_multiply_fusion
  119.5 0.0 copy-done.2
  119.5 1.7 %multiply_convert_fusion = bf16[8,12,8,1024]{3,2,1,0:T(8,128)(2,1)} fusion(bf16[8,12,8,1024]{3,2,1,0:T(8,128)(2,1)S(1)} %all-to-all-done, f32[8,12]{1,0:T(8,128)S(1)} %convert_element_type.34, f32[1024]{0:T(1024)S(1)} %copy-done.2, f32[1024]{0:T(1024)S(1)} %copy-done.1), kind=kLoop, calls=%fused_computation.2 | loop fusion | flops 4718592 | bytes 3154304 | tf_op jit(solution)/shard_map/convert_element_type | solution.py:16
  (2 shorter events, 0.0 us)
Async XLA Ops:
  3.0 11.2 %all-to-all-start.1 = ((s32[8,1,12]{2,1,0:T(1,128)}), s32[8,1,12]{2,1,0:T(1,128)S(1)}, u32[]{:S(2)}, u32[]{:S(2)}) async-start(s32[8,1,12]{2,1,0:T(1,128)} %bitcast.2), calls=%async_computation.1 | async-start | bytes 8192 | tf_op jit(solution)/shard_map/all_to_all | solution.py:44
  11.5 8.2 %copy-start = (bf16[512,1024]{1,0:T(8,128)(2,1)S(1)}, bf16[512,1024]{1,0:T(8,128)(2,1)}, u32[]{:S(2)}) copy-start(bf16[512,1024]{1,0:T(8,128)(2,1)} %param.4) | copy-start | bytes 3145732
  11.5 59.5 %copy-start.1 = (f32[1024]{0:T(1024)S(1)}, f32[1024]{0:T(1024)}, u32[]{:S(2)}) copy-start(f32[1024]{0:T(1024)} %param.6) | copy-start | bytes 12292
  14.1 56.9 %all-to-all-start = ((bf16[8,12,8,1024]{3,2,1,0:T(8,128)(2,1)}), bf16[8,12,8,1024]{3,2,1,0:T(8,128)(2,1)S(1)}, u32[]{:S(2)}, u32[]{:S(2)}) async-start(bf16[8,12,8,1024]{3,2,1,0:T(8,128)(2,1)} %bitcast.9), calls=%async_computation | async-start | bytes 3145728 | tf_op jit(solution)/shard_map/all_to_all | solution.py:43
  103.2 16.3 %copy-start.2 = (f32[1024]{0:T(1024)S(1)}, f32[1024]{0:T(1024)}, u32[]{:S(2)}) copy-start(f32[1024]{0:T(1024)} %param.7) | copy-start | bytes 12292
where the time goes:
time: 121 us
  blocking collectives  50.2 us (41%)
  local copies, waits for them, and re-layouts  36.1 us (30%)
  other arithmetic  21.2 us (18%)
  starting transfers between devices  11.7 us (10%)
    psum x1, blocking collectives, body(): within = lax.psum((sums, squares), 'shard')  44.3 us
    reshape x1, local copies, waits for them, and re-layouts, encode(): bits = bits.reshape(rows.shape[:-1] + (rows.shape[-1] // 8, 8))  31.5 us
    reduce_sum x1, other arithmetic, encode(): codes = jnp.sum(bits * weights, axis=-1) * live[..., None]  15.4 us
    all_to_all x1, starting transfers between devices, body(): lax.all_to_all(flags, 'shard', split_axis=0, concat_axis=0, tiled=True)  6.25 us
    psum x1, blocking collectives, body(): sums, squares = lax.psum((within[0], within[1]), 'group')  5.98 us
    all_to_all x1, starting transfers between devices, body(): lax.all_to_all(placed, 'shard', split_axis=0, concat_axis=0, tiled=True)  5.49 us
  transfers between devices with their start and end apart: 2, of which 1 were waited for; matrix products, arithmetic and copies ran while one was open for 4% of the time, Pallas kernels for 0%

commit v1 on v0

v1 whole, which is shorter than its diff:
```python
import functools

import jax
import jax.numpy as jnp
from jax import lax
from jax.experimental import pallas as pl
from jax.experimental.pallas import tpu as pltpu
from jax.sharding import PartitionSpec as P

BLOCK_ROWS = 8
ABSENT = 1024.0
BOUND = 64.0
MESH = pl.DeviceIdType.MESH


def kernel(
    n, groups, cap,
    emb_hbm, dest_ref, means_ref, scales_ref,
    codes_hbm, quant_hbm, stats_ref,
    emb, placed, arrived, codes, quant, weights, by_group, by_shard,
    in_sem, send_sems, recv_sems, gsend_sems, grecv_sems, ssend_sems, srecv_sems,
    codes_sems, quant_sems,
):
    g, me = lax.axis_index("group"), lax.axis_index("shard")
    rows_in, width = emb.shape
    blocks = rows_in // BLOCK_ROWS
    rows = cap * BLOCK_ROWS
    half = n // 2
    side = me // half

    load = pltpu.make_async_copy(emb_hbm, emb, in_sem)
    load.start()
    barrier = pltpu.get_barrier_semaphore()

    @pl.loop(1, n)
    def _(k):
        pl.semaphore_signal(barrier, 1, device_id=(g, lax.rem(me + k, n)), device_id_type=MESH)

    @pl.loop(1, groups)
    def _(k):
        pl.semaphore_signal(barrier, 1, device_id=(lax.rem(g + k, groups), me), device_id_type=MESH)

    owner = dest_ref[...]
    block = lax.broadcasted_iota(jnp.int32, (blocks, rows_in), 0)
    column = lax.broadcasted_iota(jnp.int32, (blocks, rows_in), 1)
    column_block = lax.shift_right_logical(column, BLOCK_ROWS.bit_length() - 1)
    owner_wide = jnp.broadcast_to(owner, (blocks, rows_in))
    owner_row = jnp.sum(jnp.where(block == column_block, owner_wide, 0), axis=0, keepdims=True)
    before = (owner_wide == owner_row) & (block < column_block)
    slot_row = jnp.sum(before.astype(jnp.int32), axis=0, keepdims=True)
    target_row = (owner_row * cap + slot_row) * BLOCK_ROWS + (column[:1] & (BLOCK_ROWS - 1))
    place = lax.broadcasted_iota(jnp.int32, (rows, rows_in), 0)
    place_row = lax.broadcasted_iota(jnp.int32, (rows, width), 0)

    def arrange(peer, out, at):
        picks = (target_row - peer * rows == place).astype(jnp.float32).astype(jnp.bfloat16)
        count = jnp.sum((owner == peer).astype(jnp.int32), axis=0, keepdims=True)
        moved = jnp.dot(picks, emb[...], preferred_element_type=jnp.float32)
        filled = place_row < jnp.broadcast_to(count * BLOCK_ROWS, (rows, width))
        out[at] = jnp.where(filled, moved, ABSENT).astype(jnp.bfloat16)

    def across(k):
        return (1 - side) * half + lax.rem(me + k, half)

    def beside(k):
        return side * half + lax.rem(me + k, half)

    def send(peer):
        return pltpu.make_async_remote_copy(
            src_ref=placed.at[peer], dst_ref=arrived.at[me],
            send_sem=send_sems.at[peer], recv_sem=recv_sems.at[me],
            device_id=(g, peer), device_id_type=MESH,
        )

    def receive(peer):
        return pltpu.make_async_remote_copy(
            src_ref=placed.at[peer], dst_ref=arrived.at[peer],
            send_sem=send_sems.at[peer], recv_sem=recv_sems.at[peer],
            device_id=(g, peer), device_id_type=MESH,
        )

    load.wait()
    first = across(0)
    arrange(first, placed, first)
    pl.semaphore_wait(barrier, n - 1 + groups - 1)
    send(first).start()

    @pl.loop(1, half)
    def _(k):
        arrange(across(k), placed, across(k))
        send(across(k)).start()

    @pl.loop(1, half)
    def _(k):
        arrange(beside(k), placed, beside(k))
        send(beside(k)).start()

    tile = 64
    total = jnp.zeros((8, width), jnp.float32)
    square = jnp.zeros((8, width), jnp.float32)

    def add(i, carry):
        total, square = carry
        x = emb[pl.ds(pl.multiple_of(i * tile, tile), tile), :].astype(jnp.float32)
        x = x.reshape(tile // 8, 8, width)
        return total + jnp.sum(x, axis=0), square + jnp.sum(x * x, axis=0)

    total, square = lax.fori_loop(0, rows_in // tile, add, (total, square))
    by_group[g, 0:1, :] = jnp.sum(total, axis=0, keepdims=True)
    by_group[g, 1:2, :] = jnp.sum(square, axis=0, keepdims=True)

    def to_group(peer, slot):
        return pltpu.make_async_remote_copy(
            src_ref=by_group.at[g], dst_ref=by_group.at[slot],
            send_sem=gsend_sems.at[peer], recv_sem=grecv_sems.at[slot],
            device_id=(peer, me), device_id_type=MESH,
        )

    def to_shard(peer, slot):
        return pltpu.make_async_remote_copy(
            src_ref=by_shard.at[me], dst_ref=by_shard.at[slot],
            send_sem=ssend_sems.at[peer], recv_sem=srecv_sems.at[slot],
            device_id=(g, peer), device_id_type=MESH,
        )

    @pl.loop(1, groups)
    def _(k):
        to_group(lax.rem(g + k, groups), g).start()

    index = lax.broadcasted_iota(jnp.int32, (width, width // 8), 0)
    byte = lax.broadcasted_iota(jnp.int32, (width, width // 8), 1)
    power = lax.shift_left(jnp.ones_like(index), index & 7)
    weights[...] = jnp.where(lax.shift_right_logical(index, 3) == byte, power, 0).astype(
        jnp.float32).astype(jnp.bfloat16)
    means = means_ref[...]
    inverse = 1.0 / scales_ref[...]
    step = 32 if rows % 32 == 0 else 16

    def write(source):
        at = pl.ds(pl.multiple_of(source * rows, rows), rows)
        return (
            pltpu.make_async_copy(codes.at[source], codes_hbm.at[at], codes_sems.at[source]),
            pltpu.make_async_copy(quant.at[source], quant_hbm.at[at], quant_sems.at[source]),
        )

    def encode(source):
        for r in range(0, rows, step):
            x = arrived[source, r:r + step, :].astype(jnp.float32)
            live = x < BOUND
            centered = x - means
            bits = jnp.where(live & (centered > 0), 1.0, 0.0).astype(jnp.bfloat16)
            scaled = jnp.clip(centered * inverse, -127.0, 127.0)
            quant[source, r:r + step, :] = jnp.where(live, scaled, 0.0).astype(jnp.bfloat16)
            packed = jnp.dot(bits, weights[...], preferred_element_type=jnp.float32)
            codes[source, r:r + step, :] = packed.astype(jnp.int32)
        for copy in write(source):
            copy.start()

    arrange(me, arrived, me)
    encode(me)

    @pl.loop(1, groups)
    def _(k):
        peer = lax.rem(g + k, groups)
        to_group(peer, peer).wait_recv()

    by_shard[me] = jnp.sum(by_group[...], axis=0)

    @pl.loop(1, n)
    def _(k):
        to_shard(lax.rem(me + k, n), me).start()

    @pl.loop(1, half)
    def _(k):
        receive(beside(k)).wait_recv()
        encode(beside(k))

    @pl.loop(1, n)
    def _(k):
        peer = lax.rem(me + k, n)
        to_shard(peer, peer).wait_recv()

    stats_ref[...] = jnp.sum(by_shard[...], axis=0)

    @pl.loop(0, half)
    def _(k):
        receive(across(k)).wait_recv()
        encode(across(k))

    @pl.loop(1, groups)
    def _(k):
        peer = lax.rem(g + k, groups)
        to_group(peer, g).wait_send()

    @pl.loop(1, n)
    def _(k):
        peer = lax.rem(me + k, n)
        send(peer).wait_send()
        to_shard(peer, me).wait_send()

    @pl.loop(0, n)
    def _(k):
        for copy in write(k):
            copy.wait()


def body(n, groups, embeddings, destinations, means, scales):
    rows_in, width = embeddings.shape
    blocks = rows_in // BLOCK_ROWS
    cap = max(2, 3 * blocks // (2 * n))
    rows = cap * BLOCK_ROWS
    hbm = pl.BlockSpec(memory_space=pl.ANY)
    vmem = pl.BlockSpec(memory_space=pltpu.VMEM)
    dma = pltpu.SemaphoreType.DMA
    return pl.pallas_call(
        functools.partial(kernel, n, groups, cap),
        out_shape=(
            jax.ShapeDtypeStruct((n * rows, width // 8), jnp.int32),
            jax.ShapeDtypeStruct((n * rows, width), jnp.bfloat16),
            jax.ShapeDtypeStruct((2, width), jnp.float32),
        ),
        in_specs=[hbm, vmem, vmem, vmem],
        out_specs=(hbm, hbm, vmem),
        scratch_shapes=[
            pltpu.VMEM((rows_in, width), jnp.bfloat16),
            pltpu.VMEM((n, rows, width), jnp.bfloat16),
            pltpu.VMEM((n, rows, width), jnp.bfloat16),
            pltpu.VMEM((n, rows, width // 8), jnp.int32),
            pltpu.VMEM((n, rows, width), jnp.bfloat16),
            pltpu.VMEM((width, width // 8), jnp.bfloat16),
            pltpu.VMEM((groups, 2, width), jnp.float32),
            pltpu.VMEM((n, 2, width), jnp.float32),
            dma(()),
            dma((n,)), dma((n,)),
            dma((groups,)), dma((groups,)),
            dma((n,)), dma((n,)),
            dma((n,)), dma((n,)),
        ],
        compiler_params=pltpu.CompilerParams(
            collective_id=0, has_side_effects=True, vmem_limit_bytes=40 * 2**20
        ),
    )(embeddings, destinations, means.reshape(1, width), scales.reshape(1, width))


def solution(mesh):
    n, groups = mesh.shape["shard"], mesh.shape["group"]
    in_specs = (P(("group", "shard"), None), P(("group", "shard"), None), P(), P())
    out_specs = (P(("group", "shard"), None), P(("group", "shard"), None), P())
    return jax.shard_map(
        functools.partial(body, n, groups),
        mesh=mesh, in_specs=in_specs, out_specs=out_specs, check_vma=False,
    )
```

time: 121 us -> 53.3 us (0.44)
  the two profiles are of different devices: /device:TPU:12 before, /device:TPU:0 now
where the time goes in v1:
time: 53.3 us; the launch traced here: 53.1 us
  Pallas kernels  46.6 us (87%)
  local copies, waits for them, and re-layouts  5.83 us (11%)
  between operations  0.64 us (1%)
    pallas_call x1, Pallas kernels, body(): pl.pallas_call(functools.partial(kernel, n, groups, cap), out_shape=(jax....  46.6 us
    unnamed x10, local copies, waits for them, and re-layouts  5.83 us

profile of v1, /device:TPU:0, one launch (start us, length us, event | category | flops | bytes accessed | tf_op | source)
XLA Modules:
  0.0 53.1 jit_solution(15247996322271544727)
XLA Ops:
  0.6 0.7 %copy.7.dest_ref = s32[64,1]{1,0:T(8,128)S(1)} copy(s32[64,1]{0,1:T(1,128)} %param.5) | data formatting | bytes 512 | tf_op args[1]
  1.4 0.0 copy-start
  1.4 1.2 %copy-done = bf16[512,1024]{1,0:T(8,128)(2,1)S(1)} copy-done((bf16[512,1024]{1,0:T(8,128)(2,1)S(1)}, bf16[512,1024]{1,0:T(8,128)(2,1)}, u32[]{:S(2)}) %copy-start) | copy-done | bytes 1048600
  2.6 0.0 copy-start.1
  2.6 0.7 %copy-done.1 = f32[1024]{0:T(1024)S(1)} copy-done((f32[1024]{0:T(1024)S(1)}, f32[1024]{0:T(1024)}, u32[]{:S(2)}) %copy-start.1) | copy-done | bytes 4120
  3.3 0.0 copy-start.2
  3.3 0.7 %copy-done.2 = f32[1024]{0:T(1024)S(1)} copy-done((f32[1024]{0:T(1024)S(1)}, f32[1024]{0:T(1024)}, u32[]{:S(2)}) %copy-start.2) | copy-done | bytes 4120
  4.0 46.6 %shard_map.67 = (s32[768,128]{1,0:T(8,128)S(1)}, bf16[768,1024]{1,0:T(8,128)(2,1)S(1)}, f32[2,1024]{1,0:T(2,128)S(1)}) custom-call(bf16[512,1024]{1,0:T(8,128)(2,1)S(1)} %copy-done, s32[64,1]{1,0:T(8,128)S(1)} %copy.7.dest_ref, f32[1,1024]{1,0:T(1,128)S(1)} %bitcast.2, f32[1,1024]{1,0:T(1,128)S(1)} %bitcast.3), custom_call_target="tpu_custom_call" | custom-call | tf_op jit(solution)/shard_map/pallas_call | solution.py:215
  50.6 0.7 %copy.11 = s32[768,128]{1,0:T(8,128)} copy(s32[768,128]{1,0:T(8,128)S(1)} %get-tuple-element.6) | data formatting | bytes 786432
  51.3 1.1 %copy.12 = bf16[768,1024]{1,0:T(8,128)(2,1)} copy(bf16[768,1024]{1,0:T(8,128)(2,1)S(1)} %get-tuple-element.7) | data formatting | bytes 3145728
  52.5 0.6 %copy.13 = f32[2,1024]{1,0:T(2,128)} copy(f32[2,1024]{1,0:T(2,128)S(1)} %get-tuple-element.8) | data formatting | bytes 16384
Async XLA Ops:
  1.4 1.2 %copy-start = (bf16[512,1024]{1,0:T(8,128)(2,1)S(1)}, bf16[512,1024]{1,0:T(8,128)(2,1)}, u32[]{:S(2)}) copy-start(bf16[512,1024]{1,0:T(8,128)(2,1)} %emb_hbm.1) | copy-start | bytes 3145732
  2.6 0.7 %copy-start.1 = (f32[1024]{0:T(1024)S(1)}, f32[1024]{0:T(1024)}, u32[]{:S(2)}) copy-start(f32[1024]{0:T(1024)} %param.6) | copy-start | bytes 12292
  3.3 0.7 %copy-start.2 = (f32[1024]{0:T(1024)S(1)}, f32[1024]{0:T(1024)}, u32[]{:S(2)}) copy-start(f32[1024]{0:T(1024)} %param.7) | copy-start | bytes 12292

commit v2 on v1

--- a/solution.py
+++ b/solution.py
@@ -15,11 +15,12 @@
 
 def kernel(
     n, groups, cap,
-    emb_hbm, dest_ref, means_ref, scales_ref,
-    codes_hbm, quant_hbm, stats_ref,
-    emb, placed, arrived, codes, quant, weights, by_group, by_shard,
-    in_sem, send_sems, recv_sems, gsend_sems, grecv_sems, ssend_sems, srecv_sems,
-    codes_sems, quant_sems,
+    emb_hbm, dest_hbm, means_hbm, scales_hbm,
+    codes_hbm, quant_hbm, stats_hbm,
+    emb, dest_ref, means_ref, scales_ref, placed, arrived, codes, quant, weights,
+    local, by_group, by_shard, whole, stats_ref,
+    in_sems, send_sems, recv_sems, gsend_sems, grecv_sems, ssend_sems, srecv_sems,
+    wsend_sems, wrecv_sems, codes_sems, quant_sems, stats_sem,
 ):
     g, me = lax.axis_index("group"), lax.axis_index("shard")
     rows_in, width = emb.shape
@@ -28,8 +29,14 @@
     half = n // 2
     side = me // half
 
-    load = pltpu.make_async_copy(emb_hbm, emb, in_sem)
-    load.start()
+    loads = [
+        pltpu.make_async_copy(source, target, in_sems.at[i])
+        for i, (source, target) in enumerate(
+            ((dest_hbm, dest_ref), (emb_hbm, emb), (means_hbm, means_ref), (scales_hbm, scales_ref))
+        )
+    ]
+    for load in loads:
+        load.start()
     barrier = pltpu.get_barrier_semaphore()
 
     @pl.loop(1, n)
@@ -40,7 +47,13 @@
     def _(k):
         pl.semaphore_signal(barrier, 1, device_id=(lax.rem(g + k, groups), me), device_id_type=MESH)
 
-    owner = dest_ref[...]
+    loads[0].wait()
+    square_block = lax.broadcasted_iota(jnp.int32, (blocks, blocks), 0)
+    square_column = lax.broadcasted_iota(jnp.int32, (blocks, blocks), 1)
+    owner_lanes = jnp.broadcast_to(dest_ref[...], (blocks, blocks))
+    owner = jnp.sum(
+        jnp.where(square_block == square_column, owner_lanes, 0), axis=1, keepdims=True
+    )
     block = lax.broadcasted_iota(jnp.int32, (blocks, rows_in), 0)
     column = lax.broadcasted_iota(jnp.int32, (blocks, rows_in), 1)
     column_block = lax.shift_right_logical(column, BLOCK_ROWS.bit_length() - 1)
@@ -60,7 +73,7 @@
         out[at] = jnp.where(filled, moved, ABSENT).astype(jnp.bfloat16)
 
     def across(k):
-        return (1 - side) * half + lax.rem(me + k, half)
+        return (1 - side) * half + (lax.rem(me, half) ^ k if half & (half - 1) == 0 else lax.rem(me + k, half))
 
     def beside(k):
         return side * half + lax.rem(me + k, half)
@@ -79,22 +92,9 @@
             device_id=(g, peer), device_id_type=MESH,
         )
 
-    load.wait()
+    loads[1].wait()
     first = across(0)
     arrange(first, placed, first)
-    pl.semaphore_wait(barrier, n - 1 + groups - 1)
-    send(first).start()
-
-    @pl.loop(1, half)
-    def _(k):
-        arrange(across(k), placed, across(k))
-        send(across(k)).start()
-
-    @pl.loop(1, half)
-    def _(k):
-        arrange(beside(k), placed, beside(k))
-        send(beside(k)).start()
-
     tile = 64
     total = jnp.zeros((8, width), jnp.float32)
     square = jnp.zeros((8, width), jnp.float32)
@@ -106,12 +106,16 @@
         return total + jnp.sum(x, axis=0), square + jnp.sum(x * x, axis=0)
 
     total, square = lax.fori_loop(0, rows_in // tile, add, (total, square))
-    by_group[g, 0:1, :] = jnp.sum(total, axis=0, keepdims=True)
-    by_group[g, 1:2, :] = jnp.sum(square, axis=0, keepdims=True)
+    part = width // groups
+    total = jnp.sum(total, axis=0, keepdims=True)
+    square = jnp.sum(square, axis=0, keepdims=True)
+    for q in range(groups):
+        local[q, 0:1, :] = total[:, q * part:(q + 1) * part]
+        local[q, 1:2, :] = square[:, q * part:(q + 1) * part]
 
     def to_group(peer, slot):
         return pltpu.make_async_remote_copy(
-            src_ref=by_group.at[g], dst_ref=by_group.at[slot],
+            src_ref=local.at[peer], dst_ref=by_group.at[slot],
             send_sem=gsend_sems.at[peer], recv_sem=grecv_sems.at[slot],
             device_id=(peer, me), device_id_type=MESH,
         )
@@ -123,15 +127,53 @@
             device_id=(g, peer), device_id_type=MESH,
         )
 
+    def to_whole(peer, slot):
+        return pltpu.make_async_remote_copy(
+            src_ref=whole.at[g], dst_ref=whole.at[slot],
+            send_sem=wsend_sems.at[peer], recv_sem=wrecv_sems.at[slot],
+            device_id=(peer, me), device_id_type=MESH,
+        )
+
+    by_group[g] = local[g]
+
+    pl.semaphore_wait(barrier, n - 1 + groups - 1)
+    send(first).start()
+
     @pl.loop(1, groups)
     def _(k):
         to_group(lax.rem(g + k, groups), g).start()
+
+    arrange(across(1), placed, across(1))
+    send(across(1)).start()
+
+    @pl.loop(1, groups)
+    def _(k):
+        peer = lax.rem(g + k, groups)
+        to_group(peer, peer).wait_recv()
+
+    by_shard[me] = jnp.sum(by_group[...], axis=0)
+
+    @pl.loop(1, n)
+    def _(k):
+        to_shard(lax.rem(me + k, n), me).start()
+
+    @pl.loop(2, half)
+    def _(k):
+        arrange(across(k), placed, across(k))
+        send(across(k)).start()
+
+    @pl.loop(1, half)
+    def _(k):
+        arrange(beside(k), placed, beside(k))
+        send(beside(k)).start()
 
     index = lax.broadcasted_iota(jnp.int32, (width, width // 8), 0)
     byte = lax.broadcasted_iota(jnp.int32, (width, width // 8), 1)
     power = lax.shift_left(jnp.ones_like(index), index & 7)
     weights[...] = jnp.where(lax.shift_right_logical(index, 3) == byte, power, 0).astype(
         jnp.float32).astype(jnp.bfloat16)
+    loads[2].wait()
+    loads[3].wait()
     means = means_ref[...]
     inverse = 1.0 / scales_ref[...]
     step = 32 if rows % 32 == 0 else 16
@@ -159,17 +201,6 @@
     arrange(me, arrived, me)
     encode(me)
 
-    @pl.loop(1, groups)
-    def _(k):
-        peer = lax.rem(g + k, groups)
-        to_group(peer, peer).wait_recv()
-
-    by_shard[me] = jnp.sum(by_group[...], axis=0)
-
-    @pl.loop(1, n)
-    def _(k):
-        to_shard(lax.rem(me + k, n), me).start()
-
     @pl.loop(1, half)
     def _(k):
         receive(beside(k)).wait_recv()
@@ -180,7 +211,11 @@
         peer = lax.rem(me + k, n)
         to_shard(peer, peer).wait_recv()
 
-    stats_ref[...] = jnp.sum(by_shard[...], axis=0)
+    whole[g] = jnp.sum(by_shard[...], axis=0)
+
+    @pl.loop(1, groups)
+    def _(k):
+        to_whole(lax.rem(g + k, groups), g).start()
 
     @pl.loop(0, half)
     def _(k):
@@ -190,7 +225,18 @@
     @pl.loop(1, groups)
     def _(k):
         peer = lax.rem(g + k, groups)
+        to_whole(peer, peer).wait_recv()
+
+    for q in range(groups):
+        stats_ref[:, q * part:(q + 1) * part] = whole[q]
+    stats_write = pltpu.make_async_copy(stats_ref, stats_hbm, stats_sem)
+    stats_write.start()
+
+    @pl.loop(1, groups)
+    def _(k):
+        peer = lax.rem(g + k, groups)
         to_group(peer, g).wait_send()
+        to_whole(peer, g).wait_send()
 
     @pl.loop(1, n)
     def _(k):
@@ -202,6 +248,8 @@
     def _(k):
         for copy in write(k):
             copy.wait()
+
+    stats_write.wait()
 
 
 def body(n, groups, embeddings, destinations, means, scales):
@@ -209,37 +257,50 @@
     blocks = rows_in // BLOCK_ROWS
     cap = max(2, 3 * blocks // (2 * n))
     rows = cap * BLOCK_ROWS
-    hbm = pl.BlockSpec(memory_space=pl.ANY)
-    vmem = pl.BlockSpec(memory_space=pltpu.VMEM)
+    anywhere = pl.BlockSpec(memory_space=pl.ANY)
     dma = pltpu.SemaphoreType.DMA
-    return pl.pallas_call(
+    part = width // groups
+    shapes = (
+        jax.ShapeDtypeStruct((n * rows, width // 8), jnp.int32),
+        jax.ShapeDtypeStruct((n * rows, width), jnp.bfloat16),
+        jax.ShapeDtypeStruct((2, width), jnp.float32),
+    )
+    results = pl.pallas_call(
         functools.partial(kernel, n, groups, cap),
-        out_shape=(
-            jax.ShapeDtypeStruct((n * rows, width // 8), jnp.int32),
-            jax.ShapeDtypeStruct((n * rows, width), jnp.bfloat16),
-            jax.ShapeDtypeStruct((2, width), jnp.float32),
-        ),
-        in_specs=[hbm, vmem, vmem, vmem],
-        out_specs=(hbm, hbm, vmem),
+        out_shape=shapes,
+        in_specs=[anywhere] * 4,
+        out_specs=(anywhere,) * 3,
         scratch_shapes=[
             pltpu.VMEM((rows_in, width), jnp.bfloat16),
+            pltpu.VMEM((1, blocks), jnp.int32),
+            pltpu.VMEM((1, width), jnp.float32),
+            pltpu.VMEM((1, width), jnp.float32),
             pltpu.VMEM((n, rows, width), jnp.bfloat16),
             pltpu.VMEM((n, rows, width), jnp.bfloat16),
             pltpu.VMEM((n, rows, width // 8), jnp.int32),
             pltpu.VMEM((n, rows, width), jnp.bfloat16),
             pltpu.VMEM((width, width // 8), jnp.bfloat16),
-            pltpu.VMEM((groups, 2, width), jnp.float32),
-            pltpu.VMEM((n, 2, width), jnp.float32),
-            dma(()),
+            pltpu.VMEM((groups, 2, part), jnp.float32),
+            pltpu.VMEM((groups, 2, part), jnp.float32),
+            pltpu.VMEM((n, 2, part), jnp.float32),
+            pltpu.VMEM((groups, 2, part), jnp.float32),
+            pltpu.VMEM((2, width), jnp.float32),
+            dma((4,)),
             dma((n,)), dma((n,)),
             dma((groups,)), dma((groups,)),
             dma((n,)), dma((n,)),
+            dma((groups,)), dma((groups,)),
             dma((n,)), dma((n,)),
+            dma(()),
         ],
         compiler_params=pltpu.CompilerParams(
             collective_id=0, has_side_effects=True, vmem_limit_bytes=40 * 2**20
         ),
-    )(embeddings, destinations, means.reshape(1, width), scales.reshape(1, width))
+    )(
+        embeddings, destinations.reshape(1, blocks),
+        means.reshape(1, width), scales.reshape(1, width),
+    )
+    return results
 
 
 def solution(mesh):

time: 53.3 us -> 47.4 us (0.89)
  the two profiles are of different devices: /device:TPU:0 before, /device:TPU:12 now
where the time goes in v2:
time: 47.4 us; the launch traced here: 46.5 us
  Pallas kernels  40.1 us (85%)
  local copies, waits for them, and re-layouts  5.73 us (12%)
  between operations  0.65 us (1%)
    pallas_call x1, Pallas kernels, body(): pl.pallas_call(functools.partial(kernel, n, groups, cap), out_shape=shape...  40.1 us
    unnamed x11, local copies, waits for them, and re-layouts  5.73 us

profile of v2, /device:TPU:12, one launch (start us, length us, event | category | flops | bytes accessed | tf_op | source)
XLA Modules:
  0.0 46.5 jit_solution(1789191515734235113)
XLA Ops:
  0.6 0.0 copy-start
  0.6 1.2 %copy-done = bf16[512,1024]{1,0:T(8,128)(2,1)S(1)} copy-done((bf16[512,1024]{1,0:T(8,128)(2,1)S(1)}, bf16[512,1024]{1,0:T(8,128)(2,1)}, u32[]{:S(2)}) %copy-start) | copy-done | bytes 1048600
  1.9 0.0 copy-start.1
  1.9 0.7 %copy-done.1 = f32[1024]{0:T(1024)S(1)} copy-done((f32[1024]{0:T(1024)S(1)}, f32[1024]{0:T(1024)}, u32[]{:S(2)}) %copy-start.1) | copy-done | bytes 4120
  2.5 0.0 copy-start.2
  2.5 0.7 %copy-done.2 = f32[1024]{0:T(1024)S(1)} copy-done((f32[1024]{0:T(1024)S(1)}, f32[1024]{0:T(1024)}, u32[]{:S(2)}) %copy-start.2) | copy-done | bytes 4120
  3.2 0.0 copy-start.3
  3.2 0.7 %copy-done.3 = s32[64,1]{0,1:T(1,128)S(1)} copy-done((s32[64,1]{0,1:T(1,128)S(1)}, s32[64,1]{0,1:T(1,128)}, u32[]{:S(2)}) %copy-start.3) | copy-done | bytes 280
  3.9 40.1 %shard_map.67 = (s32[768,128]{1,0:T(8,128)S(1)}, bf16[768,1024]{1,0:T(8,128)(2,1)S(1)}, f32[2,1024]{1,0:T(2,128)S(1)}) custom-call(bf16[512,1024]{1,0:T(8,128)(2,1)S(1)} %copy-done, s32[1,64]{1,0:T(1,128)S(1)} %bitcast.5, f32[1,1024]{1,0:T(1,128)S(1)} %bitcast.3, f32[1,1024]{1,0:T(1,128)S(1)} %bitcast.4), custom_call_target="tpu_custom_call" | custom-call | tf_op jit(solution)/shard_map/pallas_call | solution.py:268
  44.0 0.7 %copy.10 = s32[768,128]{1,0:T(8,128)} copy(s32[768,128]{1,0:T(8,128)S(1)} %get-tuple-element.6) | data formatting | bytes 786432
  44.7 1.1 %copy.11 = bf16[768,1024]{1,0:T(8,128)(2,1)} copy(bf16[768,1024]{1,0:T(8,128)(2,1)S(1)} %get-tuple-element.7) | data formatting | bytes 3145728
  45.9 0.6 %copy.12 = f32[2,1024]{1,0:T(2,128)} copy(f32[2,1024]{1,0:T(2,128)S(1)} %get-tuple-element.8) | data formatting | bytes 16384
Async XLA Ops:
  0.6 1.2 %copy-start = (bf16[512,1024]{1,0:T(8,128)(2,1)S(1)}, bf16[512,1024]{1,0:T(8,128)(2,1)}, u32[]{:S(2)}) copy-start(bf16[512,1024]{1,0:T(8,128)(2,1)} %emb_hbm.1) | copy-start | bytes 3145732
  1.9 0.7 %copy-start.1 = (f32[1024]{0:T(1024)S(1)}, f32[1024]{0:T(1024)}, u32[]{:S(2)}) copy-start(f32[1024]{0:T(1024)} %param.6) | copy-start | bytes 12292
  2.5 0.7 %copy-start.2 = (f32[1024]{0:T(1024)S(1)}, f32[1024]{0:T(1024)}, u32[]{:S(2)}) copy-start(f32[1024]{0:T(1024)} %param.7) | copy-start | bytes 12292
  3.2 0.7 %copy-start.3 = (s32[64,1]{0,1:T(1,128)S(1)}, s32[64,1]{0,1:T(1,128)}, u32[]{:S(2)}) copy-start(s32[64,1]{0,1:T(1,128)} %param.5) | copy-start | bytes 772

commit v3 on v2

--- a/solution.py
+++ b/solution.py
@@ -250,6 +250,49 @@
             copy.wait()
 
     stats_write.wait()
+
+
+def hand_over(
+    n, codes_in, quant_in, stats_in, codes_out, quant_out, stats_out,
+    codes, quant, stats, codes_load, quant_load, codes_store, quant_store, stats_sems,
+):
+    rows = codes.shape[0] // n
+
+    def steps(k):
+        at = pl.ds(pl.multiple_of(k * rows, rows), rows)
+        return (
+            pltpu.make_async_copy(quant_in.at[at], quant.at[at], quant_load.at[k]),
+            pltpu.make_async_copy(codes_in.at[at], codes.at[at], codes_load.at[k]),
+            pltpu.make_async_copy(quant.at[at], quant_out.at[at], quant_store.at[k]),
+            pltpu.make_async_copy(codes.at[at], codes_out.at[at], codes_store.at[k]),
+        )
+
+    stats_load = pltpu.make_async_copy(stats_in, stats, stats_sems.at[0])
+    stats_store = pltpu.make_async_copy(stats, stats_out, stats_sems.at[1])
+    stats_load.start()
+
+    @pl.loop(0, n)
+    def _(k):
+        for copy in steps(k)[:2]:
+            copy.start()
+
+    stats_load.wait()
+    stats_store.start()
+
+    @pl.loop(0, n)
+    def _(k):
+        load_quant, load_codes, store_quant, store_codes = steps(k)
+        load_quant.wait()
+        store_quant.start()
+        load_codes.wait()
+        store_codes.start()
+
+    stats_store.wait()
+
+    @pl.loop(0, n)
+    def _(k):
+        for copy in steps(k)[2:]:
+            copy.wait()
 
 
 def body(n, groups, embeddings, destinations, means, scales):
@@ -294,13 +337,21 @@
             dma(()),
         ],
         compiler_params=pltpu.CompilerParams(
-            collective_id=0, has_side_effects=True, vmem_limit_bytes=40 * 2**20
+            collective_id=0, has_side_effects=True, vmem_limit_bytes=58 * 2**20
         ),
     )(
         embeddings, destinations.reshape(1, blocks),
         means.reshape(1, width), scales.reshape(1, width),
     )
-    return results
+    return pl.pallas_call(
+        functools.partial(hand_over, n),
+        out_shape=shapes,
+        in_specs=[anywhere] * 3,
+        out_specs=(anywhere,) * 3,
+        scratch_shapes=[pltpu.VMEM(shape.shape, shape.dtype) for shape in shapes]
+        + [dma((n,))] * 4 + [dma((2,))],
+        compiler_params=pltpu.CompilerParams(vmem_limit_bytes=58 * 2**20),
+    )(*results)
 
 
 def solution(mesh):

time: 47.4 us -> 44.2 us (0.932); the launches traced: 46.5 us -> 43.9 us
  local copies, waits for them, and re-layouts: 5.73 us -> 0 us
  Pallas kernels: 40.1 us -> 43.2 us
    unnamed x11 -> x0, local copies, waits for them, and re-layouts: 5.73 us -> none
    pallas_call x0 -> x1, Pallas kernels: none -> 2.61 us  [body(): pl.pallas_call(functools.partial(hand_over, n), out_shape=shapes, in_spec...]
    pallas_call x1, Pallas kernels: 40.1 us -> 40.6 us  [body(): pl.pallas_call(functools.partial(kernel, n, groups, cap), out_shape=shape...]
where the time goes in v3:
time: 44.2 us; the launch traced here: 43.9 us
  Pallas kernels  43.2 us (98%)
  between operations  0.64 us (1%)
    pallas_call x1, Pallas kernels, body(): pl.pallas_call(functools.partial(kernel, n, groups, cap), out_shape=shape...  40.6 us
    pallas_call x1, Pallas kernels, body(): pl.pallas_call(functools.partial(hand_over, n), out_shape=shapes, in_spec...  2.61 us

profile of v3, /device:TPU:12, one launch (start us, length us, event | category | flops | bytes accessed | tf_op | source)
XLA Modules:
  0.0 43.9 jit_solution(13402286069883873508)
XLA Ops:
  0.6 40.6 %shard_map.67 = (s32[768,128]{1,0:T(8,128)}, bf16[768,1024]{1,0:T(8,128)(2,1)}, f32[2,1024]{1,0:T(2,128)}) custom-call(bf16[512,1024]{1,0:T(8,128)(2,1)} %emb_hbm.1, s32[1,64]{1,0:T(1,128)} %bitcast.5, f32[1,1024]{1,0:T(1,128)} %bitcast.3, f32[1,1024]{1,0:T(1,128)} %bitcast.4), custom_call_target="tpu_custom_call" | custom-call | tf_op jit(solution)/shard_map/pallas_call | solution.py:311
  41.2 2.6 %shard_map.68 = (s32[768,128]{1,0:T(8,128)}, bf16[768,1024]{1,0:T(8,128)(2,1)}, f32[2,1024]{1,0:T(2,128)}) custom-call(s32[768,128]{1,0:T(8,128)} %get-tuple-element.6.codes_in, bf16[768,1024]{1,0:T(8,128)(2,1)} %get-tuple-element.7.quant_in, f32[2,1024]{1,0:T(2,128)} %get-tuple-element.8.stats_in), custom_call_target="tpu_custom_call" | custom-call | tf_op jit(solution)/shard_map/pallas_call | solution.py:346
